TPU v7x, 256 devices: a whole 4x4x8 slice. The times are simulated.
256 devices in a mesh: expert: 128 (over z, y, x), section: 2 (over core).
Axes of the slice: x: 4, y: 4, z: 8, core: 2. Of those that a mesh axis runs over, the one named last changes fastest.
Arguments:
- tokens: bfloat16 [2048, 2048], P('expert'), may hold values from -6 to 6
- routes: int32 [2048, 8], P('expert'), may hold values from 0 to 127, all different within a row; in each aligned block of 16 rows (0 to 15, 16 to 31, ...) at most 2 rows name the same one
- route_weight: float32 [2048, 8], P('expert'), may hold values from 0.1 to 1
- moe_gain: float32 [2048], replicated, may hold values from 0.5 to 1.5
- expert_gate: bfloat16 [128, 2048, 768], P('expert', None, 'section'), may hold values from -0.125 to 0.125
- expert_up: bfloat16 [128, 2048, 768], P('expert', None, 'section'), may hold values from -0.125 to 0.125
- expert_down: bfloat16 [128, 768, 2048], P('expert', 'section'), may hold values from -0.21875 to 0.21875
- talker_proj: bfloat16 [2048, 1024], P('section'), may hold values from -0.125 to 0.125
- codebook_table: bfloat16 [2, 2048, 1024], P('section'), may hold values from -6 to 6
- level_gain: float32 [2, 1024], P('section'), may hold values from 0.5 to 1.5
- earlier_codes: int32 [2048], P('expert'), may hold values from 0 to 2047
Outputs:
- hidden_out: bfloat16 [2048, 2048], P('expert', 'section')
- logits: bfloat16 [2048, 2, 2048], P('expert', 'section')
Inputs may be any that keep to these rules, and one draw needn't show every extreme that they name: Among the rows of one index of expert, no expert is named by more than 2 of the 8 routes of its tokens, and some expert reaches 2; a token names 8 different experts.
All inputs are finite; a program needn't handle non-finite values.
Results may differ from a plain program's by a relative error of at most 0.012.
Values may be sent and summed in bfloat16 or wider, within the bound.
A program may use at most 64 MiB of HBM per device.

v0:
```python
import math

import jax
import jax.numpy as jnp
from jax import lax
from jax.sharding import PartitionSpec as P


def swapped(value, axis, apart):
    mask = 2**apart
    pairs = [(source, source ^ mask) for source in range(lax.axis_size(axis))]
    return lax.ppermute(value, axis, pairs)


def passed_along(value, axis, steps):
    count = lax.axis_size(axis)
    initial, last = (max(0, -steps), min(count, count - steps))
    return lax.ppermute(value, axis, [(source, source + steps) for source in range(initial, last)])


def rms_scale(values, gain_row):
    mean_square = jnp.mean(values * values, axis=-1, keepdims=True) + 1e-06
    return values * lax.rsqrt(mean_square) * gain_row


def shards(
    tokens,
    routes,
    route_weight,
    moe_gain,
    expert_gate,
    expert_up,
    expert_down,
    talker_proj,
    codebook_table,
    level_gain,
    earlier_codes,
):
    tok_count, model_width = tokens.shape
    top_count = routes.shape[1]
    experts_all = lax.axis_size("expert") * expert_gate.shape[0]
    capacity = max(2, 2 * tok_count * top_count // experts_all)
    section_index = lax.axis_index("section")
    half_width = model_width // lax.axis_size("section")
    gate_w = expert_gate[0]
    up_w = expert_up[0]
    down_w = expert_down[0]
    normed = rms_scale(tokens.astype(jnp.float32), moe_gain).astype(jnp.bfloat16)
    shares = route_weight / jnp.sum(route_weight, axis=1, keepdims=True)
    route_flat = routes.reshape(-1)
    expert_ids = jnp.arange(experts_all, dtype=jnp.int32)
    onehot = (route_flat[:, None] == expert_ids[None, :]).astype(jnp.int32)
    earlier_hits = jnp.cumsum(onehot, axis=0) - onehot
    slot_index = jnp.sum(earlier_hits * onehot, axis=1)
    target_row = route_flat * capacity + slot_index
    token_of = jnp.arange(tok_count * top_count, dtype=jnp.int32) // top_count
    outgoing = (
        jnp.zeros((experts_all * capacity, model_width), jnp.bfloat16)
        .at[target_row]
        .set(normed[token_of])
    )
    outgoing = outgoing.reshape(experts_all, capacity, model_width)
    incoming = lax.all_to_all(outgoing, "expert", split_axis=0, concat_axis=0, tiled=True)
    flat_rows = incoming.reshape(-1, model_width)
    gate_val = jnp.dot(flat_rows, gate_w, preferred_element_type=jnp.float32)
    up_val = jnp.dot(flat_rows, up_w, preferred_element_type=jnp.float32)
    hidden_units = (jax.nn.silu(gate_val) * up_val).astype(jnp.bfloat16)
    partial_value = jnp.dot(hidden_units, down_w, preferred_element_type=jnp.float32)
    partial_value = partial_value.reshape(incoming.shape)
    partner = swapped(partial_value.astype(jnp.bfloat16), "section", 0).astype(partial_value.dtype)
    finished = (partial_value + partner).astype(jnp.bfloat16)
    returned = lax.all_to_all(finished, "expert", split_axis=0, concat_axis=0, tiled=True)
    picked = returned.reshape(-1, model_width)[target_row].astype(jnp.float32)
    weighted = picked.reshape(tok_count, top_count, model_width) * shares[:, :, None]
    mixture = jnp.sum(weighted, axis=1)
    complete = (tokens.astype(jnp.float32) + mixture).astype(jnp.bfloat16)
    hidden_half = lax.dynamic_slice_in_dim(complete, section_index * half_width, half_width, 1)
    partial_talk = jnp.dot(hidden_half, talker_proj, preferred_element_type=jnp.float32)
    talk = lax.psum(partial_talk, "section")
    code_table = codebook_table[0]
    gain_row = level_gain[0]
    predictor_width = code_table.shape[1]
    sent_level = talk + code_table[earlier_codes].astype(jnp.float32)
    received = passed_along(sent_level, "section", 1)
    level_input = jnp.where(section_index == 0, talk, received)
    level_normed = rms_scale(level_input, gain_row).astype(jnp.bfloat16)
    scores = lax.dot_general(
        level_normed, code_table, (((1,), (1,)), ((), ())), preferred_element_type=jnp.float32
    )
    logits = (scores / math.sqrt(predictor_width)).astype(jnp.bfloat16)[:, None, :]
    return (hidden_half, logits)


def solution(mesh):
    in_specs = (
        P("expert", None),
        P("expert", None),
        P("expert", None),
        P(),
        P("expert", None, "section"),
        P("expert", None, "section"),
        P("expert", "section", None),
        P("section", None),
        P("section", None, None),
        P("section", None),
        P("expert"),
    )
    out_specs = (P("expert", "section"), P("expert", "section", None))
    return jax.shard_map(shards, mesh=mesh, in_specs=in_specs, out_specs=out_specs, check_vma=False)
```

profile of v0, /device:TPU:1, one launch (start us, length us, event | category | flops | bytes accessed | tf_op | source)
XLA Modules:
  0.0 158.3 jit_solution(1123645189339317123)
XLA Ops:
  7.2 0.0 copy-start
  7.2 0.8 broadcast_multiply_fusion
  8.0 0.8 copy.23
  8.8 0.1 copy.22
  8.8 0.1 mul.79
  8.9 0.1 eq.18
  9.0 0.1 fusion.20
  9.1 0.2 reduce_window_sum.11
  9.3 0.2 select_reduce_fusion
  9.5 1.0 multiply_reduce_fusion
  10.5 0.9 multiply_convert_fusion
  11.4 3.4 %scatter_custom_fusion = bf16[256,2048]{1,0:T(8,128)(2,1)S(1)} fusion(s32[128]{0:T(128)S(1)} %get-tuple-element.5, bf16[16,2048]{1,0:T(8,128)(2,1)S(1)} %multiply_convert_fusion, s32[1024]{0:T(1024)S(1)} %pad_clamp_fusion.2, bf16[]{:T(256)} %constant.18.clone.1), kind=kCustom, calls=%fused_computation.18 | custom fusion | bytes 1048578 | tf_op jit(solution)/shard_map/scatter | solution.py:60
  14.8 1.5 reshape.111
  16.3 45.0 %all_to_all.10 = bf16[128,2,2048]{2,1,0:T(2,128)(2,1)} all-to-all(bf16[128,2,2048]{2,1,0:T(2,128)(2,1)} %reshape.111), channel_id=1, replica_groups=mesh['expert'=128,'section'=2] {'expert'}, dimensions={0} | all-to-all | bytes 2097152 | tf_op jit(solution)/shard_map/all_to_all | solution.py:63
  61.4 1.5 reshape.112
  62.8 0.0 copy-start.5
  62.8 2.2 %fusion.6 = f32[256,384]{1,0:T(8,128)S(1)} fusion(bf16[256,2048]{1,0:T(8,128)(2,1)S(1)} %reshape.112, bf16[1,2048,384]{2,1,0:T(8,128)(2,1)} %param.15), kind=kOutput, calls=%fused_computation.12 | convolution fusion | flops 402653184 | bytes 3014656 | tf_op jit(solution)/shard_map/dot_general | solution.py:65
  65.1 0.0 copy-done.5
  65.1 0.7 fusion.11
  65.8 0.1 dot_general.19
  65.9 2.1 %fusion.26 = (bf16[128,2,2048]{2,0,1:T(8,128)(2,1)S(1)}, f32[128,2,2048]{2,0,1:T(8,128)S(1)}) fusion(bf16[1,384,2048]{2,1,0:T(8,128)(2,1)} %param.17, bf16[128,2,384]{2,1,0:T(2,128)(2,1)S(1)} %dot_general.19), kind=kOutput, calls=%fused_computation.53 | convolution fusion | flops 403177472 | bytes 4915200 | tf_op jit(solution)/shard_map/dot_general | solution.py:68
  68.0 3.6 %collective-permute-start = (bf16[128,2,2048]{2,0,1:T(8,128)(2,1)S(1)}, bf16[128,2,2048]{2,0,1:T(8,128)(2,1)S(1)}, u32[]{:S(2)}, u32[]{:S(2)}) collective-permute-start(bf16[128,2,2048]{2,0,1:T(8,128)(2,1)S(1)} %get-tuple-element.2), channel_id=1, source_target_pairs={{0,1},{1,0},{2,3},{3,2},{4,5},{5,4},{6,7},{7,6},{8,9},{9,8},{10,11... | collective-permute-start | bytes 3145736 | tf_op jit(solution)/shard_map/ppermute | solution.py:12
  71.6 2.3 %collective-permute-done = bf16[128,2,2048]{2,0,1:T(8,128)(2,1)S(1)} collective-permute-done((bf16[128,2,2048]{2,0,1:T(8,128)(2,1)S(1)}, bf16[128,2,2048]{2,0,1:T(8,128)(2,1)S(1)}, u32[]{:S(2)}, u32[]{:S(2)}) %collective-permute-start) | collective-permute-done | bytes 1048608 | tf_op jit(solution)/shard_map/ppermute | solution.py:12
  73.9 0.3 add_convert_fusion
  74.2 0.0 copy-start.1
  74.2 0.0 copy-start.3
  74.2 0.0 copy-start.6
  74.2 2.1 %copy.25 = bf16[128,2,2048]{2,1,0:T(2,128)(2,1)} copy(bf16[128,2,2048]{2,0,1:T(8,128)(2,1)S(1)} %add_convert_fusion) | data formatting | bytes 2097152 | tf_op jit(solution)/shard_map/convert_element_type | solution.py:71
  76.4 7.5 %all-to-all-start.1 = ((bf16[128,2,2048]{2,1,0:T(2,128)(2,1)}), bf16[128,2,2048]{2,1,0:T(2,128)(2,1)}, u32[]{:S(2)}, u32[]{:S(2)}) async-start(bf16[128,2,2048]{2,1,0:T(2,128)(2,1)} %copy.25), calls=%async_computation.1 | async-start | bytes 2097152 | tf_op jit(solution)/shard_map/all_to_all | solution.py:72
  83.9 0.0 all-reduce.2.cloned.1.call-start
  83.9 0.0 copy-done.1
  83.9 0.0 copy-done.3
  84.0 0.1 copy.26
  84.1 28.9 %all-to-all-done.1 = bf16[128,2,2048]{2,1,0:T(2,128)(2,1)} async-done(((bf16[128,2,2048]{2,1,0:T(2,128)(2,1)}), bf16[128,2,2048]{2,1,0:T(2,128)(2,1)}, u32[]{:S(2)}, u32[]{:S(2)}) %all-to-all-start.1) | async-done | bytes 1048608 | tf_op jit(solution)/shard_map/all_to_all | solution.py:72
  113.0 1.5 reshape.113
  114.5 1.7 %gather_fusion = bf16[128,2048]{1,0:T(8,128)(2,1)} fusion(bf16[256,2048]{1,0:T(8,128)(2,1)S(1)} %reshape.113, s32[1024]{0:T(1024)S(1)} %pad_clamp_fusion.1), kind=kCustom, calls=%fused_computation.1 | custom fusion | bytes 1049088 | tf_op jit(solution)/shard_map/gather | solution.py:73
  116.2 1.5 fusion.14
  117.7 0.0 copy-start.2
  117.8 1.0 fusion.27
  118.8 0.0 all-reduce.2.cloned.1.call-update
  118.8 3.3 %gather_fusion.1 = bf16[16,1024]{1,0:T(8,128)(2,1)S(1)} fusion(bf16[2048,1024]{1,0:T(8,128)(2,1)} %bitcast.37, s32[1024]{0:T(1024)S(1)} %pad_clamp_fusion), kind=kCustom, calls=%fused_computation.2 | custom fusion | bytes 65600 | tf_op jit(solution)/shard_map/gather | solution.py:83
  122.2 21.1 %all-reduce.2.cloned.1.call-done = f32[16,1024]{1,0:T(8,128)} async-done(((f32[16,1024]{1,0:T(8,128)}), f32[16,1024]{1,0:T(8,128)}) %all-reduce.2.cloned.1.call-update) | async-done | bytes 65552 | tf_op jit(solution)/shard_map/psum | solution.py:79
  143.3 0.8 convert_add_fusion
  144.2 1.3 collective-permute-start.1
  145.4 1.8 %collective-permute-done.1 = f32[16,1024]{1,0:T(8,128)S(1)} collective-permute-done((f32[16,1024]{1,0:T(8,128)S(1)}, f32[16,1024]{1,0:T(8,128)S(1)}, u32[]{:S(2)}, u32[]{:S(2)}) %collective-permute-start.1) | collective-permute-done | bytes 65568 | tf_op jit(solution)/shard_map/ppermute | solution.py:18
  147.3 0.1 multiply_reduce_fusion.1
  147.4 4.0 %fusion.1 = bf16[16,1,2048]{2,0,1:T(8,128)(2,1)} fusion(f32[1024]{0:T(1024)S(1)} %bitcast.38, f32[16]{0:T(128)S(1)} %add_rsqrt_fusion, f32[16,1024]{1,0:T(8,128)} %all-reduce.2.cloned.1.call-done, f32[16,1024]{1,0:T(8,128)S(1)} %collective-permute-done.1, pred[]{:T(512)S(6)} %eq.22, bf16[1,2048,1024]{2,1,0:T(8,128)(2,1)} %param.19), kind=kOutput, calls=%fused_computation.6 | convolution fusion | flops 67239936 | bytes 4395073 | tf_op jit(solution)/shard_map/dot_general | solution.py:87
  151.5 0.0 copy-done.2
  (15 shorter events, 0.1 us)
Async XLA Ops:
  7.2 110.6 %copy-start = (bf16[1024,1024]{1,0:T(8,128)(2,1)S(1)}, bf16[1024,1024]{1,0:T(8,128)(2,1)}, u32[]{:S(2)}) copy-start(bf16[1024,1024]{1,0:T(8,128)(2,1)} %param.18) | copy-start | bytes 6291460
  62.8 2.2 %copy-start.5 = (bf16[1,2048,384]{2,1,0:T(8,128)(2,1)S(1)}, bf16[1,2048,384]{2,1,0:T(8,128)(2,1)}, u32[]{:S(2)}) copy-start(bf16[1,2048,384]{2,1,0:T(8,128)(2,1)} %param.16) | copy-start | bytes 4718596
  68.0 5.9 %collective-permute-start = (bf16[128,2,2048]{2,0,1:T(8,128)(2,1)S(1)}, bf16[128,2,2048]{2,0,1:T(8,128)(2,1)S(1)}, u32[]{:S(2)}, u32[]{:S(2)}) collective-permute-start(bf16[128,2,2048]{2,0,1:T(8,128)(2,1)S(1)} %get-tuple-element.2), channel_id=1, source_target_pairs={{0,1},{1,0},{2,3},{3,2},{4,5},{5,4},{6,7},{7,6},{8,9},{9,8},{10,11... | collective-permute-start | bytes 3145736 | tf_op jit(solution)/shard_map/ppermute | solution.py:12
  74.2 9.7 %copy-start.1 = (bf16[16,2048]{1,0:T(8,128)(2,1)S(1)}, bf16[16,2048]{1,0:T(8,128)(2,1)}, u32[]{:S(2)}) copy-start(bf16[16,2048]{1,0:T(8,128)(2,1)} %param.11) | copy-start | bytes 196612
  74.2 9.7 %copy-start.3 = (f32[16,8]{0,1:T(8,128)S(1)}, f32[16,8]{0,1:T(8,128)}, u32[]{:S(2)}) copy-start(f32[16,8]{0,1:T(8,128)} %param.13) | copy-start | bytes 1540
  74.2 9.8 %copy-start.6 = (s32[16]{0:T(128)S(1)}, s32[16]{0:T(128)}, u32[]{:S(2)}) copy-start(s32[16]{0:T(128)} %param.21) | copy-start | bytes 196
  76.4 36.6 %all-to-all-start.1 = ((bf16[128,2,2048]{2,1,0:T(2,128)(2,1)}), bf16[128,2,2048]{2,1,0:T(2,128)(2,1)}, u32[]{:S(2)}, u32[]{:S(2)}) async-start(bf16[128,2,2048]{2,1,0:T(2,128)(2,1)} %copy.25), calls=%async_computation.1 | async-start | bytes 2097152 | tf_op jit(solution)/shard_map/all_to_all | solution.py:72
  83.9 59.4 %all-reduce.2.cloned.1.call-start = ((), (), s32[]{:S(2)}) async-start(), calls=%async_computation.2 | async-start | bytes 131072 | tf_op jit(solution)/shard_map/psum | solution.py:79
  116.2 31.2 %copy-start.4 = (f32[1,1024]{1,0:T(1,128)S(1)}, f32[1,1024]{1,0:T(1,128)}, u32[]{:S(2)}) copy-start(f32[1,1024]{1,0:T(1,128)} %param.20) | copy-start | bytes 12292
  117.7 33.7 %copy-start.2 = (bf16[16,1024]{1,0:T(8,128)(2,1)}, bf16[16,1024]{1,0:T(8,128)(2,1)S(1)}, u32[]{:S(2)}) copy-start(bf16[16,1024]{1,0:T(8,128)(2,1)S(1)} %fusion.19) | copy-start | bytes 98308
  144.2 3.1 %collective-permute-start.1 = (f32[16,1024]{1,0:T(8,128)S(1)}, f32[16,1024]{1,0:T(8,128)S(1)}, u32[]{:S(2)}, u32[]{:S(2)}) collective-permute-start(f32[16,1024]{1,0:T(8,128)S(1)} %convert_add_fusion), channel_id=1, source_target_pairs={{0,1},{2,3},{4,5},{6,7},{8,9},{10,11},{12,13},{14,15},{16,17},{18,... | collective-permute-start | bytes 196616 | tf_op jit(solution)/shard_map/ppermute | solution.py:18
Sparse Core Ops, SparseCore 0:
  118.9 24.3 all-reduce.1
where the time goes:
time: 159 us; the launch traced here: 158 us
  waiting for transfers between devices  54.2 us (34%)
  blocking collectives  45 us (28%)
  local copies, waits for them, and re-layouts  16.2 us (10%)
  between operations  14.3 us (9%)
  starting transfers between devices  12.4 us (8%)
  matrix products  10.1 us (6%)
  other arithmetic  6.05 us (4%)
    all_to_all x1, blocking collectives, shards(): lax.all_to_all(outgoing, 'expert', split_axis=0, concat_axis=0, tiled=True)  45 us
    all_to_all x1, waiting for transfers between devices, shards(): lax.all_to_all(finished, 'expert', split_axis=0, concat_axis=0, tiled=True)  28.9 us
    psum x1, waiting for transfers between devices, shards(): talk = lax.psum(partial_talk, 'section')  21.1 us
    all_to_all x1, starting transfers between devices, shards(): lax.all_to_all(finished, 'expert', split_axis=0, concat_axis=0, tiled=True)  7.5 us
    dot_general x1, matrix products, shards(): lax.dot_general(level_normed, code_table, (((1,), (1,)), ((), ())), prefe...  4.04 us
    ppermute x1, starting transfers between devices, swapped(): return lax.ppermute(value, axis, pairs)  3.62 us
    scatter x1, local copies, waits for them, and re-layouts, shards(): outgoing = jnp.zeros((experts_all * capacity, model_width), jnp.bfloat16)...  3.36 us
    gather x1, local copies, waits for them, and re-layouts, shards(): sent_level = talk + code_table[earlier_codes].astype(jnp.float32)  3.34 us
  transfers between devices with their start and end apart: 4, of which 4 were waited for; matrix products, arithmetic and copies ran while one was open for 2% of the time, Pallas kernels for 0%

commit v1 on v0

v1 whole, which is shorter than its diff:
```python
import functools

import jax
import jax.numpy as jnp
from jax import lax
from jax.experimental import pallas as pl
from jax.experimental.pallas import tpu as pltpu
from jax.sharding import PartitionSpec as P

MESH = pl.DeviceIdType.MESH
NZ, NY, NX = 8, 4, 4
CAP = 2
CHUNKS = 2
GROUPS = 4
META = 128
BF, F32 = jnp.bfloat16, jnp.float32


def kernel(
    tokens_hbm, routes_hbm, weight_hbm, gain_hbm, gate_hbm, up_hbm, down_hbm, proj_hbm, table_hbm, lgain_hbm, codes,
    hidden_out, logits_out,
    tok, rts, rwt, gain, lgain, wgu, wd, wp, tb,
    zbuf, sel, recv, part, acc, psend, precv, own, outb, ret, zout, zin, wmix, emb, tsend, trecv,
    load_sem, z_s, z_r, p_s, p_r, f_s, f_r, q_s, q_r, r_s, r_r, u_s, u_r, t_s, t_r,
):
    plane = NY * NX
    rows, width = tok.shape
    half = width // 2
    ff = gate_hbm.shape[2]
    top = rts.shape[1]
    experts = NZ * plane
    cw = half // CHUNKS
    slots = plane * NZ * CAP
    span = NZ * CAP
    stream = NZ * rows
    me = lax.axis_index("expert")
    sec = lax.axis_index("section")
    x, y, z = me % NX, (me // NX) % NY, me // plane
    other = 1 - sec

    def at_plane(dy, dx):
        return z * plane + ((y + dy) % NY) * NX + (x + dx) % NX

    def at_z(dz):
        return ((z + dz) % NZ) * plane + y * NX + x

    forth = [(o, at_plane(o // NX, o % NX)) for o in range(1, plane)]
    back = [(o, at_plane(NY - o // NX, NX - o % NX)) for o in range(1, plane)]

    pairs = [
        (tokens_hbm, tok),
        (routes_hbm, rts),
        (weight_hbm, rwt),
        (gain_hbm, gain),
        (lgain_hbm, lgain),
        (gate_hbm.at[0, pl.ds(sec * half, half), :], wgu.at[0, :, 0:ff]),
        (up_hbm.at[0, pl.ds(sec * half, half), :], wgu.at[0, :, ff : 2 * ff]),
        (gate_hbm.at[0, pl.ds(other * half, half), :], wgu.at[1, :, 0:ff]),
        (up_hbm.at[0, pl.ds(other * half, half), :], wgu.at[1, :, ff : 2 * ff]),
        (down_hbm.at[0, :, pl.ds(other * half, half)], wd.at[1]),
        (down_hbm.at[0, :, pl.ds(sec * half, half)], wd.at[0]),
        (table_hbm.at[0], tb),
        (proj_hbm, wp),
    ]
    loads = [pltpu.make_async_copy(src, dst, load_sem.at[i]) for i, (src, dst) in enumerate(pairs)]
    for load in loads:
        load.start()

    barrier = pltpu.get_barrier_semaphore()
    for d in range(1, NZ):
        pl.semaphore_signal(barrier, inc=1, device_id=(at_z(d), sec), device_id_type=MESH)
    for _, peer in forth:
        pl.semaphore_signal(barrier, inc=1, device_id=(peer, sec), device_id_type=MESH)
    pl.semaphore_signal(barrier, inc=1, device_id=(me, other), device_id_type=MESH)

    for i in range(4):
        loads[i].wait()
    routes = rts[...]
    expert_lane = lax.broadcasted_iota(jnp.int32, (rows, experts), 1)
    named = [routes[:, k : k + 1] == expert_lane for k in range(top)]
    hit = functools.reduce(jnp.logical_or, named)
    below = lax.broadcasted_iota(jnp.int32, (rows, rows), 0) > lax.broadcasted_iota(jnp.int32, (rows, rows), 1)
    earlier = jnp.dot(below.astype(F32).astype(BF), hit.astype(F32).astype(BF), preferred_element_type=F32)
    weight = rwt[...]
    shares = weight / jnp.sum(weight, axis=1, keepdims=True)
    shares_hi = shares.astype(BF).astype(F32)
    shares_lo = shares - shares_hi
    lane = lax.broadcasted_iota(jnp.int32, (rows, META), 1)
    meta = jnp.zeros((rows, META), F32)
    for k in range(top):
        rank = jnp.sum(jnp.where(named[k], earlier, 0.0), axis=1, keepdims=True)
        target = routes[:, k : k + 1].astype(F32) * CAP + rank
        meta = jnp.where(lane == k, target, meta)
        meta = jnp.where(lane == top + k, shares_hi[:, k : k + 1], meta)
        meta = jnp.where(lane == 2 * top + k, shares_lo[:, k : k + 1], meta)
    zbuf[0, :, 0:META] = meta.astype(BF)
    values = tok[...].astype(F32)
    scale = lax.rsqrt(jnp.mean(values * values, axis=1, keepdims=True) + 1e-06)
    mine = tok[:, pl.ds(sec * half, half)].astype(F32)
    zbuf[0, :, META:] = (mine * scale * gain[:, pl.ds(sec * half, half)]).astype(BF)

    pl.semaphore_wait(barrier, NZ - 1 + plane - 1 + 1)

    def z_lanes(c):
        return pl.ds(0, META + cw) if c == 0 else pl.ds(META + c * cw, cw)

    def z_copy(c, src, dst, device):
        return pltpu.make_async_remote_copy(
            src_ref=zbuf.at[src, :, z_lanes(c)], dst_ref=zbuf.at[dst, :, z_lanes(c)],
            send_sem=z_s.at[c], recv_sem=z_r.at[c], device_id=(device, sec), device_id_type=MESH,
        )

    for c in range(CHUNKS):
        for d in range(1, NZ):
            z_copy(c, 0, d, at_z(d)).start()

    slot = lax.broadcasted_iota(jnp.int32, (slots, 1), 0)
    slot_o, slot_d, slot_s = slot // span, (slot // CAP) % NZ, slot % CAP
    slot_expert = z * plane + ((y + slot_o // NX) % NY) * NX + (x + slot_o % NX) % NX
    slot_target = (slot_expert * CAP + slot_s).astype(F32)
    same_block = slot_d == lax.broadcasted_iota(jnp.int32, (slots, stream), 1) // rows

    def plane_copy(c, src, dst, peer, o, send, get):
        return pltpu.make_async_remote_copy(
            src_ref=src.at[c, o], dst_ref=dst.at[c, o], send_sem=send, recv_sem=get,
            device_id=(peer, sec), device_id_type=MESH,
        )

    per = plane // GROUPS
    for c in range(CHUNKS):
        z_copy(c, pl.ds(1, NZ - 1), pl.ds(1, NZ - 1), me).wait_recv()
        if c == 0:
            columns = zbuf[:, :, 0:META].reshape(stream, META).astype(F32)
            across = columns.T
            pick = functools.reduce(jnp.logical_or, [across[k : k + 1, :] == slot_target for k in range(top)])
            pick = jnp.logical_and(pick, same_block).astype(F32).astype(BF)
        features = zbuf[:, :, META + c * cw : META + (c + 1) * cw].reshape(stream, cw)
        chosen = jnp.dot(pick, features, preferred_element_type=F32).astype(BF).reshape(plane, span, cw)
        sel[c] = chosen
        recv[c, 0] = chosen[0]
        for o, peer in forth:
            plane_copy(c, sel, recv, peer, o, p_s.at[c], p_r.at[c, o // per]).start()

    lane_slot = lax.broadcasted_iota(jnp.int32, (1, slots), 1)
    lane_o = lane_slot // span
    lane_expert = z * plane + ((y + lane_o // NX) % NY) * NX + (x + lane_o % NX) % NX
    lane_target = (lane_expert * CAP + lane_slot % CAP).astype(F32)
    lane_block = (lane_slot // CAP) % NZ == lax.broadcasted_iota(jnp.int32, (stream, slots), 0) // rows
    hi = jnp.zeros((stream, slots), F32)
    lo = jnp.zeros((stream, slots), F32)
    for k in range(top):
        here = jnp.logical_and(columns[:, k : k + 1] == lane_target, lane_block)
        hi = jnp.where(here, columns[:, top + k : top + k + 1], hi)
        lo = jnp.where(here, columns[:, 2 * top + k : 2 * top + k + 1], lo)
    wmix[0:stream] = hi.astype(BF)
    wmix[stream:] = lo.astype(BF)

    vocabulary = tb.shape[0]
    column = jnp.zeros((rows, 1), jnp.int32)
    row_at = lax.broadcasted_iota(jnp.int32, (rows, 1), 0)
    for i in range(rows):
        column = jnp.where(row_at == i, codes[i], column)
    code_hit = (column == lax.broadcasted_iota(jnp.int32, (rows, vocabulary), 1)).astype(F32).astype(BF)
    loads[11].wait()
    emb[...] = jnp.dot(code_hit, tb[...], preferred_element_type=F32)

    def core_copy(src, dst, send, get):
        return pltpu.make_async_remote_copy(
            src_ref=src, dst_ref=dst, send_sem=send, recv_sem=get, device_id=(me, other), device_id_type=MESH
        )

    for i in range(5, 9):
        loads[i].wait()
    for c in range(CHUNKS):
        for g in range(GROUPS):
            block = pl.ds(max(g * per, 1), (g + 1) * per - max(g * per, 1))
            plane_copy(c, sel, recv, me, block, p_s.at[c], p_r.at[c, g]).wait_recv()
            group = pl.ds(g * per, per)
            core_copy(recv.at[c, group], part.at[c, group], f_s.at[c], f_r.at[c]).start()
        product = jnp.dot(recv[c].reshape(slots, cw), wgu[0, c * cw : (c + 1) * cw, :], preferred_element_type=F32)
        acc[...] = product if c == 0 else acc[...] + product
    for c in range(CHUNKS):
        core_copy(recv.at[c], part.at[c], f_s.at[c], f_r.at[c]).wait_recv()
        acc[...] += jnp.dot(part[c].reshape(slots, cw), wgu[1, c * cw : (c + 1) * cw, :], preferred_element_type=F32)
    gate_val = acc[:, 0:ff]
    units = (gate_val / (1.0 + jnp.exp(-gate_val)) * acc[:, ff:]).astype(BF)

    loads[9].wait()
    for c in range(CHUNKS):
        partial = jnp.dot(units, wd[1, :, c * cw : (c + 1) * cw], preferred_element_type=F32)
        psend[c] = partial.astype(BF)
        core_copy(psend.at[c], precv.at[c], q_s.at[c], q_r.at[c]).start()
    loads[10].wait()
    for c in range(CHUNKS):
        own[c] = jnp.dot(units, wd[0, :, c * cw : (c + 1) * cw], preferred_element_type=F32)
    for c in range(CHUNKS):
        core_copy(psend.at[c], precv.at[c], q_s.at[c], q_r.at[c]).wait_recv()
        finished = (own[c] + precv[c].astype(F32)).astype(BF).reshape(plane, span, cw)
        outb[c] = finished
        ret[c, 0] = finished[0]
        for o, peer in back:
            plane_copy(c, outb, ret, peer, o, r_s.at[c], r_r.at[c]).start()

    for c in range(CHUNKS):
        z_copy(c, pl.ds(1, NZ - 1), pl.ds(1, NZ - 1), me).wait_send()
        plane_copy(c, sel, recv, me, pl.ds(1, plane - 1), p_s.at[c], p_r.at[c, 0]).wait_send()
        core_copy(recv.at[c], part.at[c], f_s.at[c], f_r.at[c]).wait_send()

    def u_copy(c, d, device):
        return pltpu.make_async_remote_copy(
            src_ref=zout.at[c, d], dst_ref=zin.at[c, d], send_sem=u_s.at[c], recv_sem=u_r.at[c],
            device_id=(device, sec), device_id_type=MESH,
        )

    everyone = pl.ds(1, plane - 1)
    for c in range(CHUNKS):
        plane_copy(c, outb, ret, me, everyone, r_s.at[c], r_r.at[c]).wait_recv()
        both = jnp.dot(wmix[...], ret[c].reshape(slots, cw), preferred_element_type=F32)
        summed = (both[0:stream] + both[stream:]).astype(BF).reshape(NZ, rows, cw)
        zout[c] = summed
        zin[c, 0] = summed[0]
        for d in range(1, NZ):
            u_copy(c, d, at_z(NZ - d)).start()

    loads[12].wait()
    loads[4].wait()
    partial_talk = None
    for c in range(CHUNKS):
        u_copy(c, pl.ds(1, NZ - 1), me).wait_recv()
        mixture = functools.reduce(jnp.add, [zin[c, d].astype(F32) for d in range(NZ)])
        at = pl.multiple_of(sec * half + c * cw, cw)
        complete = (tok[:, pl.ds(at, cw)].astype(F32) + mixture).astype(BF)
        hidden_out[:, c * cw : (c + 1) * cw] = complete
        product = jnp.dot(complete, wp[c * cw : (c + 1) * cw, :], preferred_element_type=F32)
        partial_talk = product if partial_talk is None else partial_talk + product
    tsend[...] = partial_talk + jnp.where(sec == 0, emb[...], 0.0)
    talk_copy = core_copy(tsend, trecv, t_s, t_r)
    talk_copy.start()
    for c in range(CHUNKS):
        core_copy(psend.at[c], precv.at[c], q_s.at[c], q_r.at[c]).wait_send()
        plane_copy(c, outb, ret, me, everyone, r_s.at[c], r_r.at[c]).wait_send()
        u_copy(c, pl.ds(1, NZ - 1), me).wait_send()
    talk_copy.wait()

    level = partial_talk + trecv[...]
    level_scale = lax.rsqrt(jnp.mean(level * level, axis=1, keepdims=True) + 1e-06)
    level_normed = (level * level_scale * lgain[...]).astype(BF)
    scores = lax.dot_general(level_normed, tb[...], (((1,), (1,)), ((), ())), preferred_element_type=F32)
    logits_out[...] = (scores / (level.shape[1] ** 0.5)).astype(BF)


def shards(
    tokens,
    routes,
    route_weight,
    moe_gain,
    expert_gate,
    expert_up,
    expert_down,
    talker_proj,
    codebook_table,
    level_gain,
    earlier_codes,
):
    rows, width = tokens.shape
    top = routes.shape[1]
    half, plane = width // 2, NY * NX
    ff = expert_gate.shape[2]
    vocabulary, talk_width = codebook_table.shape[1:]
    cw = half // CHUNKS
    span, stream = NZ * CAP, NZ * rows
    slots = plane * span
    chunk = (CHUNKS, plane, span, cw)
    dma = pltpu.SemaphoreType.DMA
    anywhere = pl.BlockSpec(memory_space=pl.ANY)
    vmem = pl.BlockSpec(memory_space=pltpu.VMEM)
    hidden, logits = pl.pallas_call(
        kernel,
        out_shape=(
            jax.ShapeDtypeStruct((rows, half), BF),
            jax.ShapeDtypeStruct((rows, vocabulary), BF),
        ),
        in_specs=[anywhere] * 10 + [pl.BlockSpec(memory_space=pltpu.SMEM)],
        out_specs=(vmem, vmem),
        scratch_shapes=[
            pltpu.VMEM((rows, width), BF),
            pltpu.VMEM((rows, top), jnp.int32),
            pltpu.VMEM((rows, top), F32),
            pltpu.VMEM((1, width), F32),
            pltpu.VMEM((1, talk_width), F32),
            pltpu.VMEM((2, half, 2 * ff), BF),
            pltpu.VMEM((2, ff, half), BF),
            pltpu.VMEM((half, talk_width), BF),
            pltpu.VMEM((vocabulary, talk_width), BF),
            pltpu.VMEM((NZ, rows, META + half), BF),
            pltpu.VMEM(chunk, BF),
            pltpu.VMEM(chunk, BF),
            pltpu.VMEM(chunk, BF),
            pltpu.VMEM((slots, 2 * ff), F32),
            pltpu.VMEM((CHUNKS, slots, cw), BF),
            pltpu.VMEM((CHUNKS, slots, cw), BF),
            pltpu.VMEM((CHUNKS, slots, cw), F32),
            pltpu.VMEM(chunk, BF),
            pltpu.VMEM(chunk, BF),
            pltpu.VMEM((CHUNKS, NZ, rows, cw), BF),
            pltpu.VMEM((CHUNKS, NZ, rows, cw), BF),
            pltpu.VMEM((2 * stream, slots), BF),
            pltpu.VMEM((rows, talk_width), F32),
            pltpu.VMEM((rows, talk_width), F32),
            pltpu.VMEM((rows, talk_width), F32),
            dma((13,)),
            dma((CHUNKS,)),
            dma((CHUNKS,)),
            dma((CHUNKS,)),
            dma((CHUNKS, GROUPS)),
            dma((CHUNKS,)),
            dma((CHUNKS,)),
            dma((CHUNKS,)),
            dma((CHUNKS,)),
            dma((CHUNKS,)),
            dma((CHUNKS,)),
            dma((CHUNKS,)),
            dma((CHUNKS,)),
            dma,
            dma,
        ],
        compiler_params=pltpu.CompilerParams(
            collective_id=0, has_side_effects=True, vmem_limit_bytes=60 * 1024 * 1024
        ),
        name="expert_step",
    )(
        tokens,
        routes,
        route_weight,
        moe_gain.reshape(1, width),
        expert_gate,
        expert_up,
        expert_down,
        talker_proj,
        codebook_table,
        level_gain,
        earlier_codes,
    )
    return hidden, logits[:, None, :]


def solution(mesh):
    in_specs = (
        P("expert", None),
        P("expert", None),
        P("expert", None),
        P(),
        P("expert", None, "section"),
        P("expert", None, "section"),
        P("expert", "section", None),
        P("section", None),
        P("section", None, None),
        P("section", None),
        P("expert"),
    )
    out_specs = (P("expert", "section"), P("expert", "section", None))
    return jax.shard_map(shards, mesh=mesh, in_specs=in_specs, out_specs=out_specs, check_vma=False)
```

time: 159 us -> 55.8 us (0.35)
  waiting for transfers between devices: 54.2 us -> 0 us
  Pallas kernels: 0 us -> 49.3 us
  blocking collectives: 45 us -> 0 us
  between operations: 14.3 us -> 0.64 us
  starting transfers between devices: 12.4 us -> 0 us
  local copies, waits for them, and re-layouts: 16.2 us -> 5.56 us
  matrix products: 10.1 us -> 0 us
  other arithmetic: 6.05 us -> 0 us
    pallas_call x0 -> x1, Pallas kernels: none -> 49.3 us  [shards(): pl.pallas_call(kernel, out_shape=(jax.ShapeDtypeStruct((rows, half), BF),...]
    all_to_all x1 -> x0, blocking collectives: 45 us -> none  [shards(): lax.all_to_all(outgoing, 'expert', split_axis=0, concat_axis=0, tiled=True)]
    all_to_all x1 -> x0, waiting for transfers between devices: 28.9 us -> none  [shards(): lax.all_to_all(finished, 'expert', split_axis=0, concat_axis=0, tiled=True)]
    psum x1 -> x0, waiting for transfers between devices: 21.1 us -> none  [shards(): talk = lax.psum(partial_talk, 'section')]
    dot_general x5 -> x0, matrix products: 10.1 us -> none  [the longest x1 4.04 us: shards(): lax.dot_general(level_normed, code_table, (((1,), (1,)), ((), ())), prefe...]
    all_to_all x1 -> x0, starting transfers between devices: 7.5 us -> none  [shards(): lax.all_to_all(finished, 'expert', split_axis=0, concat_axis=0, tiled=True)]
    gather x2 -> x0, local copies, waits for them, and re-layouts: 5.06 us -> none  [the longest x1 3.34 us: shards(): sent_level = talk + code_table[earlier_codes].astype(jnp.float32)]
    ppermute x2 -> x0, starting transfers between devices: 4.9 us -> none  [the longest x1 3.62 us: swapped(): return lax.ppermute(value, axis, pairs)]
  transfers between devices with their start and end apart: 4 -> 0, of which waited for: 4 -> 0; matrix products, arithmetic and copies ran while one was open for 2% -> 0% of each run, Pallas kernels for 0% -> 0%
where the time goes in v1:
time: 55.8 us; the launch traced here: 55.5 us
  Pallas kernels  49.3 us (88%)
  local copies, waits for them, and re-layouts  5.56 us (10%)
  between operations  0.64 us (1%)
    pallas_call x1, Pallas kernels, shards(): pl.pallas_call(kernel, out_shape=(jax.ShapeDtypeStruct((rows, half), BF),...  49.3 us
    unnamed x4, local copies, waits for them, and re-layouts  5.56 us

profile of v1, /device:TPU:1, one launch (start us, length us, event | category | flops | bytes accessed | tf_op | source)
XLA Modules:
  0.0 55.5 jit_solution(1840261372532916331)
XLA Ops:
  0.6 1.4 %copy.13.routes_hbm = s32[16,8]{1,0:T(8,128)} copy(s32[16,8]{0,1:T(8,128)} %param.12) | data formatting | bytes 1024 | tf_op args[1]
  2.0 1.4 %copy.14.weight_hbm = f32[16,8]{1,0:T(8,128)} copy(f32[16,8]{0,1:T(8,128)} %param.13) | data formatting | bytes 1024 | tf_op args[2]
  3.3 49.3 %expert_step.1 = (bf16[16,1024]{1,0:T(8,128)(2,1)}, bf16[16,2048]{1,0:T(8,128)(2,1)}) custom-call(bf16[16,2048]{1,0:T(8,128)(2,1)} %tokens_hbm.1, s32[16,8]{1,0:T(8,128)} %copy.13.routes_hbm, f32[16,8]{1,0:T(8,128)} %copy.14.weight_hbm, f32[1,2048]{1,0:T(1,128)} %bitcast.3, bf16[1,2048,384]{2,1,0:T(8,128)(2,1)} %gate_hbm.1, bf16[1,2048,384]{2,1,0:T(8,128)(2,1)} %up_hbm.1, ...), custom_call_target="tpu_custom_call" | custom-call | tf_op jit(solution)/shard_map/expert_step/pallas_call | solution.py:277
  52.7 1.4 %copy.17 = bf16[16,1024]{1,0:T(8,128)(2,1)} copy(bf16[16,1024]{1,0:T(8,128)(2,1)} %get-tuple-element.8) | data formatting | bytes 65536
  54.1 1.5 %copy.18 = bf16[16,1,2048]{2,0,1:T(8,128)(2,1)} copy(bf16[16,1,2048]{2,0,1:T(8,128)(2,1)} %bitcast.2) | data formatting | bytes 131072

commit v2 on v1

v2 whole, which is shorter than its diff:
```python
import functools

import jax
import jax.numpy as jnp
from jax import lax
from jax.experimental import pallas as pl
from jax.experimental.pallas import tpu as pltpu
from jax.sharding import PartitionSpec as P

MESH = pl.DeviceIdType.MESH
NZ, NY, NX = 8, 4, 4
CAP = 2
CHUNKS = 4
BF, F32 = jnp.bfloat16, jnp.float32


def kernel(
    tokens_hbm, routes_hbm, weight_hbm, gain_hbm, gate_hbm, up_hbm, down_hbm, proj_hbm, table_hbm, lgain_hbm, codes_hbm,
    hidden_out, level_out, tb,
    codes, tok, rts, rwt, gain, lgain, wgu, wd, wp,
    mbuf, zbuf, sel, recv, part, acc, psend, precv, own, outb, ret, zout, zin, wmix, emb, tsend, trecv,
    load_sem, m_s, m_r, z_s, z_r, p_s, p_r, f_s, f_r, q_s, q_r, r_s, r_r, u_s, u_r, t_s, t_r,
):
    plane = NY * NX
    rows, width = tok.shape
    half = width // 2
    ff = gate_hbm.shape[2]
    top = rts.shape[0]
    cw = half // CHUNKS
    slots = plane * NZ * CAP
    span = NZ * CAP
    stream = NZ * rows
    named = top * rows
    pairs_all = NZ * named
    me = lax.axis_index("expert")
    sec = lax.axis_index("section")
    x, y, z = me % NX, (me // NX) % NY, me // plane
    other = 1 - sec

    def at_plane(dy, dx):
        return z * plane + ((y + dy) % NY) * NX + (x + dx) % NX

    def at_z(dz):
        return ((z + dz) % NZ) * plane + y * NX + x

    forth = [(o, at_plane(o // NX, o % NX)) for o in range(1, plane)]
    back = [(o, at_plane(NY - o // NX, NX - o % NX)) for o in range(1, plane)]

    barrier = pltpu.get_barrier_semaphore()
    for d in range(1, NZ):
        pl.semaphore_signal(barrier, inc=1, device_id=(at_z(d), sec), device_id_type=MESH)
    for _, peer in forth:
        pl.semaphore_signal(barrier, inc=1, device_id=(peer, sec), device_id_type=MESH)
    pl.semaphore_signal(barrier, inc=1, device_id=(me, other), device_id_type=MESH)

    pairs = [
        (tokens_hbm, tok),
        (routes_hbm, rts),
        (weight_hbm, rwt),
        (gain_hbm, gain),
        (lgain_hbm, lgain),
        (gate_hbm.at[0, pl.ds(sec * half, half), :], wgu.at[0, :, 0:ff]),
        (up_hbm.at[0, pl.ds(sec * half, half), :], wgu.at[0, :, ff : 2 * ff]),
        (gate_hbm.at[0, pl.ds(other * half, half), :], wgu.at[1, :, 0:ff]),
        (up_hbm.at[0, pl.ds(other * half, half), :], wgu.at[1, :, ff : 2 * ff]),
        (down_hbm.at[0, :, pl.ds(other * half, half)], wd.at[1]),
        (down_hbm.at[0, :, pl.ds(sec * half, half)], wd.at[0]),
        (table_hbm.at[0], tb),
        (proj_hbm, wp),
        (codes_hbm, codes),
    ]
    loads = [pltpu.make_async_copy(src, dst, load_sem.at[i]) for i, (src, dst) in enumerate(pairs)]
    for load in loads:
        load.start()

    for i in range(4):
        loads[i].wait()
    tiled = jnp.concatenate([rts[...]] * top, axis=1)
    weights = jnp.concatenate([rwt[...]] * top, axis=1)
    lane = lax.broadcasted_iota(jnp.int32, (top, named), 1)
    diagonal = lane // rows == lax.broadcasted_iota(jnp.int32, (top, named), 0)
    route = jnp.sum(jnp.where(diagonal, tiled, 0), axis=0, keepdims=True)
    rank = jnp.zeros((top, named), jnp.int32)
    for step in range(1, rows):
        same = jnp.logical_and(pltpu.roll(tiled, step, 1) == route, lane % rows >= step)
        rank += same.astype(jnp.int32)
    target = route * CAP + jnp.sum(rank, axis=0, keepdims=True)
    total = jnp.sum(weights, axis=0, keepdims=True)
    mbuf[0, 0:1, :] = target.astype(F32)
    mbuf[0, 1:2, :] = jnp.sum(jnp.where(diagonal, weights, 0.0), axis=0, keepdims=True) / total
    values = tok[...].astype(F32)
    scale = lax.rsqrt(jnp.mean(values * values, axis=1, keepdims=True) + 1e-06)
    mine = tok[:, pl.ds(sec * half, half)].astype(F32)
    mine = (mine * scale * gain[:, pl.ds(sec * half, half)]).astype(BF)
    for c in range(CHUNKS):
        zbuf[c, 0] = mine[:, c * cw : (c + 1) * cw]

    pl.semaphore_wait(barrier, NZ - 1 + plane - 1 + 1)

    def m_copy(dst, device):
        return pltpu.make_async_remote_copy(
            src_ref=mbuf.at[0] if isinstance(dst, int) else mbuf.at[dst], dst_ref=mbuf.at[dst],
            send_sem=m_s, recv_sem=m_r, device_id=(device, sec), device_id_type=MESH,
        )

    def z_copy(c, src, dst, device):
        return pltpu.make_async_remote_copy(
            src_ref=zbuf.at[c, src], dst_ref=zbuf.at[c, dst],
            send_sem=z_s.at[c], recv_sem=z_r.at[c], device_id=(device, sec), device_id_type=MESH,
        )

    others = pl.ds(1, NZ - 1)
    for d in range(1, NZ):
        m_copy(d, at_z(d)).start()
    for c in range(CHUNKS):
        for d in range(1, NZ):
            z_copy(c, 0, d, at_z(d)).start()

    slot = lax.broadcasted_iota(jnp.int32, (slots, 1), 0)
    slot_o, slot_d, slot_s = slot // span, (slot // CAP) % NZ, slot % CAP
    slot_expert = z * plane + ((y + slot_o // NX) % NY) * NX + (x + slot_o % NX) % NX
    block_base = NZ * plane * CAP
    slot_target = (slot_expert * CAP + slot_s + slot_d * block_base).astype(F32)

    def plane_copy(c, src, dst, peer, o, send, get):
        return pltpu.make_async_remote_copy(
            src_ref=src.at[c, o], dst_ref=dst.at[c, o], send_sem=send, recv_sem=get,
            device_id=(peer, sec), device_id_type=MESH,
        )

    m_copy(others, me).wait_recv()
    hits = [mbuf[d, 0:1, :] + float(d * block_base) == slot_target for d in range(NZ)]
    pick = jnp.concatenate([hit.astype(F32).astype(BF) for hit in hits], axis=1)
    for c in range(CHUNKS):
        z_copy(c, others, others, me).wait_recv()
        features = jnp.concatenate([zbuf[c, d // top] for d in range(NZ * top)], axis=0)
        chosen = jnp.dot(pick, features, preferred_element_type=F32).astype(BF).reshape(plane, span, cw)
        sel[c] = chosen
        recv[c, 0] = chosen[0]
        for o, peer in forth:
            plane_copy(c, sel, recv, peer, o, p_s.at[c], p_r.at[c]).start()

    weighted = jnp.concatenate(
        [jnp.where(hit, mbuf[d, 1:2, :], 0.0) for d, hit in enumerate(hits)], axis=1
    )
    weighted_hi = weighted.astype(BF)
    weighted_lo = (weighted - weighted_hi.astype(F32)).astype(BF)
    pair = lax.broadcasted_iota(jnp.int32, (pairs_all, stream), 0)
    row_of = (pair // named) * rows + pair % rows
    fold = (row_of == lax.broadcasted_iota(jnp.int32, (pairs_all, stream), 1)).astype(F32).astype(BF)
    across = jnp.dot(weighted_hi, fold, preferred_element_type=F32).T
    wmix[0:stream] = across.astype(BF)
    across = jnp.dot(weighted_lo, fold, preferred_element_type=F32).T
    wmix[stream:] = across.astype(BF)

    vocabulary = tb.shape[0]
    column = jnp.zeros((rows, 1), jnp.int32)
    row_at = lax.broadcasted_iota(jnp.int32, (rows, 1), 0)
    loads[13].wait()
    for i in range(rows):
        column = jnp.where(row_at == i, codes[i], column)
    code_hit = (column == lax.broadcasted_iota(jnp.int32, (rows, vocabulary), 1)).astype(F32).astype(BF)
    loads[11].wait()
    emb[...] = jnp.dot(code_hit, tb[...], preferred_element_type=F32)

    def core_copy(src, dst, send, get):
        return pltpu.make_async_remote_copy(
            src_ref=src, dst_ref=dst, send_sem=send, recv_sem=get, device_id=(me, other), device_id_type=MESH
        )

    everyone = pl.ds(1, plane - 1)
    for i in range(5, 9):
        loads[i].wait()
    for c in range(CHUNKS):
        plane_copy(c, sel, recv, me, everyone, p_s.at[c], p_r.at[c]).wait_recv()
        core_copy(recv.at[c], part.at[c], f_s.at[c], f_r.at[c]).start()
        product = jnp.dot(recv[c].reshape(slots, cw), wgu[0, c * cw : (c + 1) * cw, :], preferred_element_type=F32)
        acc[...] = product if c == 0 else acc[...] + product
    for c in range(CHUNKS):
        core_copy(recv.at[c], part.at[c], f_s.at[c], f_r.at[c]).wait_recv()
        acc[...] += jnp.dot(part[c].reshape(slots, cw), wgu[1, c * cw : (c + 1) * cw, :], preferred_element_type=F32)
    gate_val = acc[:, 0:ff]
    units = (gate_val / (1.0 + jnp.exp(-gate_val)) * acc[:, ff:]).astype(BF)

    loads[9].wait()
    for c in range(CHUNKS):
        partial = jnp.dot(units, wd[1, :, c * cw : (c + 1) * cw], preferred_element_type=F32)
        psend[c] = partial.astype(BF)
        core_copy(psend.at[c], precv.at[c], q_s.at[c], q_r.at[c]).start()
    loads[10].wait()
    for c in range(CHUNKS):
        own[c] = jnp.dot(units, wd[0, :, c * cw : (c + 1) * cw], preferred_element_type=F32)
    for c in range(CHUNKS):
        core_copy(psend.at[c], precv.at[c], q_s.at[c], q_r.at[c]).wait_recv()
        finished = (own[c] + precv[c].astype(F32)).astype(BF).reshape(plane, span, cw)
        outb[c] = finished
        ret[c, 0] = finished[0]
        for o, peer in back:
            plane_copy(c, outb, ret, peer, o, r_s.at[c], r_r.at[c]).start()

    m_copy(others, me).wait_send()
    for c in range(CHUNKS):
        z_copy(c, others, others, me).wait_send()
        plane_copy(c, sel, recv, me, everyone, p_s.at[c], p_r.at[c]).wait_send()
        core_copy(recv.at[c], part.at[c], f_s.at[c], f_r.at[c]).wait_send()

    def u_copy(c, d, device):
        return pltpu.make_async_remote_copy(
            src_ref=zout.at[c, d], dst_ref=zin.at[c, d], send_sem=u_s.at[c], recv_sem=u_r.at[c],
            device_id=(device, sec), device_id_type=MESH,
        )

    for c in range(CHUNKS):
        plane_copy(c, outb, ret, me, everyone, r_s.at[c], r_r.at[c]).wait_recv()
        both = jnp.dot(wmix[...], ret[c].reshape(slots, cw), preferred_element_type=F32)
        summed = (both[0:stream] + both[stream:]).astype(BF).reshape(NZ, rows, cw)
        zout[c] = summed
        zin[c, 0] = summed[0]
        for d in range(1, NZ):
            u_copy(c, d, at_z(NZ - d)).start()

    loads[12].wait()
    loads[4].wait()
    partial_talk = None
    for c in range(CHUNKS):
        u_copy(c, others, me).wait_recv()
        mixture = functools.reduce(jnp.add, [zin[c, d].astype(F32) for d in range(NZ)])
        at = pl.multiple_of(sec * half + c * cw, cw)
        complete = (tok[:, pl.ds(at, cw)].astype(F32) + mixture).astype(BF)
        hidden_out[:, c * cw : (c + 1) * cw] = complete
        product = jnp.dot(complete, wp[c * cw : (c + 1) * cw, :], preferred_element_type=F32)
        partial_talk = product if partial_talk is None else partial_talk + product
    tsend[...] = partial_talk + jnp.where(sec == 0, emb[...], 0.0)
    talk_copy = core_copy(tsend, trecv, t_s, t_r)
    talk_copy.start()
    for c in range(CHUNKS):
        core_copy(psend.at[c], precv.at[c], q_s.at[c], q_r.at[c]).wait_send()
        plane_copy(c, outb, ret, me, everyone, r_s.at[c], r_r.at[c]).wait_send()
        u_copy(c, others, me).wait_send()
    talk_copy.wait()

    level = partial_talk + trecv[...]
    level_scale = lax.rsqrt(jnp.mean(level * level, axis=1, keepdims=True) + 1e-06)
    level_out[...] = (level * level_scale * lgain[...]).astype(BF)


def head(hidden, level_normed, table, hidden_hbm, logits_hbm, logits, sems):
    hidden_copy = pltpu.make_async_copy(hidden, hidden_hbm, sems.at[0])
    hidden_copy.start()
    scores = lax.dot_general(level_normed[...], table[...], (((1,), (1,)), ((), ())), preferred_element_type=F32)
    logits[...] = (scores / (table.shape[1] ** 0.5)).astype(BF)
    logits_copy = pltpu.make_async_copy(logits, logits_hbm, sems.at[1])
    logits_copy.start()
    hidden_copy.wait()
    logits_copy.wait()


def shards(
    tokens,
    routes,
    route_weight,
    moe_gain,
    expert_gate,
    expert_up,
    expert_down,
    talker_proj,
    codebook_table,
    level_gain,
    earlier_codes,
):
    rows, width = tokens.shape
    top = routes.shape[1]
    half, plane = width // 2, NY * NX
    ff = expert_gate.shape[2]
    vocabulary, talk_width = codebook_table.shape[1:]
    cw = half // CHUNKS
    span, stream = NZ * CAP, NZ * rows
    slots = plane * span
    chunk = (CHUNKS, plane, span, cw)
    dma = pltpu.SemaphoreType.DMA
    hbm = pl.BlockSpec(memory_space=pltpu.HBM)
    vmem = pl.BlockSpec(memory_space=pltpu.VMEM)
    operands = (
        tokens,
        routes.T,
        route_weight.T,
        moe_gain.reshape(1, width),
        expert_gate,
        expert_up,
        expert_down,
        talker_proj,
        codebook_table,
        level_gain,
        earlier_codes,
    )
    hidden, level_normed, table = pl.pallas_call(
        kernel,
        out_shape=(
            pltpu.VMEM((rows, half), BF),
            pltpu.VMEM((rows, talk_width), BF),
            pltpu.VMEM((vocabulary, talk_width), BF),
        ),
        in_specs=[hbm] * 11,
        out_specs=(vmem,) * 3,
        scratch_shapes=[
            pltpu.SMEM((rows,), jnp.int32),
            pltpu.VMEM((rows, width), BF),
            pltpu.VMEM((top, rows), jnp.int32),
            pltpu.VMEM((top, rows), F32),
            pltpu.VMEM((1, width), F32),
            pltpu.VMEM((1, talk_width), F32),
            pltpu.VMEM((2, half, 2 * ff), BF),
            pltpu.VMEM((2, ff, half), BF),
            pltpu.VMEM((half, talk_width), BF),
            pltpu.VMEM((NZ, 2, top * rows), F32),
            pltpu.VMEM((CHUNKS, NZ, rows, cw), BF),
            pltpu.VMEM(chunk, BF),
            pltpu.VMEM(chunk, BF),
            pltpu.VMEM(chunk, BF),
            pltpu.VMEM((slots, 2 * ff), F32),
            pltpu.VMEM((CHUNKS, slots, cw), BF),
            pltpu.VMEM((CHUNKS, slots, cw), BF),
            pltpu.VMEM((CHUNKS, slots, cw), F32),
            pltpu.VMEM(chunk, BF),
            pltpu.VMEM(chunk, BF),
            pltpu.VMEM((CHUNKS, NZ, rows, cw), BF),
            pltpu.VMEM((CHUNKS, NZ, rows, cw), BF),
            pltpu.VMEM((2 * stream, slots), BF),
            pltpu.VMEM((rows, talk_width), F32),
            pltpu.VMEM((rows, talk_width), F32),
            pltpu.VMEM((rows, talk_width), F32),
            dma((14,)),
            dma,
            dma,
            dma((CHUNKS,)),
            dma((CHUNKS,)),
            dma((CHUNKS,)),
            dma((CHUNKS,)),
            dma((CHUNKS,)),
            dma((CHUNKS,)),
            dma((CHUNKS,)),
            dma((CHUNKS,)),
            dma((CHUNKS,)),
            dma((CHUNKS,)),
            dma((CHUNKS,)),
            dma((CHUNKS,)),
            dma,
            dma,
        ],
        compiler_params=pltpu.CompilerParams(
            collective_id=0, has_side_effects=True, vmem_limit_bytes=36 * 1024 * 1024
        ),
        name="expert_step",
    )(*[pltpu.with_memory_space_constraint(operand, pltpu.HBM) for operand in operands])
    hidden, logits = pl.pallas_call(
        head,
        out_shape=(
            jax.ShapeDtypeStruct((rows, half), BF),
            jax.ShapeDtypeStruct((rows, vocabulary), BF),
        ),
        in_specs=[vmem] * 3,
        out_specs=(hbm, hbm),
        scratch_shapes=[pltpu.VMEM((rows, vocabulary), BF), dma((2,))],
        compiler_params=pltpu.CompilerParams(vmem_limit_bytes=16 * 1024 * 1024),
        name="head",
    )(hidden, level_normed, table)
    return hidden, logits[:, None, :]


def solution(mesh):
    in_specs = (
        P("expert", None),
        P("expert", None),
        P("expert", None),
        P(),
        P("expert", None, "section"),
        P("expert", None, "section"),
        P("expert", "section", None),
        P("section", None),
        P("section", None, None),
        P("section", None),
        P("expert"),
    )
    out_specs = (P("expert", "section"), P("expert", "section", None))
    return jax.shard_map(shards, mesh=mesh, in_specs=in_specs, out_specs=out_specs, check_vma=False)
```

time: 55.8 us -> 46.9 us (0.84)
  local copies, waits for them, and re-layouts: 5.56 us -> 0 us
  Pallas kernels: 49.3 us -> 46.2 us
    unnamed x4 -> x0, local copies, waits for them, and re-layouts: 5.56 us -> none
    pallas_call x1 -> x2, Pallas kernels: 49.3 us -> 46.2 us  [the longest x1 44.3 us: shards(): pl.pallas_call(kernel, out_shape=(pltpu.VMEM((rows, half), BF), pltpu.VME...]
where the time goes in v2:
time: 46.9 us; the launch traced here: 46.8 us
  Pallas kernels  46.2 us (99%)
  between operations  0.64 us (1%)
    pallas_call x1, Pallas kernels, shards(): pl.pallas_call(kernel, out_shape=(pltpu.VMEM((rows, half), BF), pltpu.VME...  44.3 us
    pallas_call x1, Pallas kernels, shards(): pl.pallas_call(head, out_shape=(jax.ShapeDtypeStruct((rows, half), BF), j...  1.85 us

profile of v2, /device:TPU:1, one launch (start us, length us, event | category | flops | bytes accessed | tf_op | source)
XLA Modules:
  0.0 46.8 jit_solution(17645100167001508345)
XLA Ops:
  0.6 44.3 %expert_step.1 = (bf16[16,1024]{1,0:T(8,128)(2,1)S(1)}, bf16[16,1024]{1,0:T(8,128)(2,1)S(1)}, bf16[2048,1024]{1,0:T(8,128)(2,1)S(1)}) custom-call(bf16[16,2048]{1,0:T(8,128)(2,1)} %tokens_hbm.1, s32[8,16]{1,0:T(8,128)} %bitcast.5, f32[8,16]{1,0:T(8,128)} %bitcast.6, f32[1,2048]{1,0:T(1,128)} %bitcast.4, bf16[1,2048,384]{2,1,0:T(8,128)(2,1)} %gate_hbm.1, ...), custom_call_target="tpu_custom_call" | custom-call | tf_op jit(solution)/shard_map/expert_step/pallas_call | solution.py:296
  45.0 1.9 %head.1 = (bf16[16,1024]{1,0:T(8,128)(2,1)}, bf16[16,2048]{1,0:T(8,128)(2,1)}) custom-call(bf16[16,1024]{1,0:T(8,128)(2,1)S(1)} %get-tuple-element.7.hidden, bf16[16,1024]{1,0:T(8,128)(2,1)S(1)} %get-tuple-element.8.level_normed, bf16[2048,1024]{1,0:T(8,128)(2,1)S(1)} %get-tuple-element.9.table), custom_call_target="tpu_custom_call" | custom-call | tf_op jit(solution)/shard_map/head/pallas_call | solution.py:355

commit v3 on v2

--- a/solution.py
+++ b/solution.py
@@ -18,8 +18,8 @@
     tokens_hbm, routes_hbm, weight_hbm, gain_hbm, gate_hbm, up_hbm, down_hbm, proj_hbm, table_hbm, lgain_hbm, codes_hbm,
     hidden_out, level_out, tb,
     codes, tok, rts, rwt, gain, lgain, wgu, wd, wp,
-    mbuf, zbuf, sel, recv, part, acc, psend, precv, own, outb, ret, zout, zin, wmix, emb, tsend, trecv,
-    load_sem, m_s, m_r, z_s, z_r, p_s, p_r, f_s, f_r, q_s, q_r, r_s, r_r, u_s, u_r, t_s, t_r,
+    mbuf, zbuf, sel, recv, acc, outb, ret, zout, zin, wmix, emb, tsend, trecv,
+    load_sem, m_s, m_r, z_s, z_r, p_s, p_r, e_s, w_s, w_r, r_s, r_r, g_s, u_s, u_r, t_s, t_r,
 ):
     plane = NY * NX
     rows, width = tok.shape
@@ -43,34 +43,51 @@
     def at_z(dz):
         return ((z + dz) % NZ) * plane + y * NX + x
 
-    forth = [(o, at_plane(o // NX, o % NX)) for o in range(1, plane)]
-    back = [(o, at_plane(NY - o // NX, NX - o % NX)) for o in range(1, plane)]
-
-    barrier = pltpu.get_barrier_semaphore()
-    for d in range(1, NZ):
-        pl.semaphore_signal(barrier, inc=1, device_id=(at_z(d), sec), device_id_type=MESH)
-    for _, peer in forth:
-        pl.semaphore_signal(barrier, inc=1, device_id=(peer, sec), device_id_type=MESH)
-    pl.semaphore_signal(barrier, inc=1, device_id=(me, other), device_id_type=MESH)
-
+    def apart(step, count):
+        return min(step, count - step)
+
+    offsets = sorted(range(1, plane), key=lambda o: -apart(o // NX, NY) - apart(o % NX, NX))
+    forth = [(o, at_plane(o // NX, o % NX)) for o in offsets]
+    z_steps = sorted(range(1, NZ), key=lambda d: -apart(d, NZ))
+
+    hidden_columns = pl.ds(sec * ff, ff)
+    up_columns = pl.ds(2 * ff + sec * ff, ff)
     pairs = [
         (tokens_hbm, tok),
         (routes_hbm, rts),
         (weight_hbm, rwt),
         (gain_hbm, gain),
         (lgain_hbm, lgain),
-        (gate_hbm.at[0, pl.ds(sec * half, half), :], wgu.at[0, :, 0:ff]),
-        (up_hbm.at[0, pl.ds(sec * half, half), :], wgu.at[0, :, ff : 2 * ff]),
-        (gate_hbm.at[0, pl.ds(other * half, half), :], wgu.at[1, :, 0:ff]),
-        (up_hbm.at[0, pl.ds(other * half, half), :], wgu.at[1, :, ff : 2 * ff]),
-        (down_hbm.at[0, :, pl.ds(other * half, half)], wd.at[1]),
-        (down_hbm.at[0, :, pl.ds(sec * half, half)], wd.at[0]),
+        (gate_hbm.at[0], wgu.at[:, hidden_columns]),
+        (up_hbm.at[0], wgu.at[:, up_columns]),
+        (down_hbm.at[0], wd.at[hidden_columns]),
         (table_hbm.at[0], tb),
         (proj_hbm, wp),
         (codes_hbm, codes),
     ]
     loads = [pltpu.make_async_copy(src, dst, load_sem.at[i]) for i, (src, dst) in enumerate(pairs)]
-    for load in loads:
+    for load in loads[:4]:
+        load.start()
+
+    barrier = pltpu.get_barrier_semaphore()
+
+    def greet(device, core):
+        pl.semaphore_signal(barrier, inc=1, device_id=(device, core), device_id_type=MESH)
+
+    for d in z_steps:
+        greet(at_z(d), sec)
+    for o, peer in forth:
+        greet(peer, o % 2)
+    greet(me, other)
+    for parity in range(2):
+
+        @pl.when(sec == parity)
+        def _():
+            for o, peer in forth:
+                if o % 2 == parity:
+                    greet(peer, 1 - parity)
+
+    for load in loads[4:]:
         load.start()
 
     for i in range(4):
@@ -95,7 +112,7 @@
     for c in range(CHUNKS):
         zbuf[c, 0] = mine[:, c * cw : (c + 1) * cw]
 
-    pl.semaphore_wait(barrier, NZ - 1 + plane - 1 + 1)
+    pl.semaphore_wait(barrier, NZ - 1 + plane - 1 + 1 + plane // 2 - 1 + sec)
 
     def m_copy(dst, device):
         return pltpu.make_async_remote_copy(
@@ -110,11 +127,20 @@
         )
 
     others = pl.ds(1, NZ - 1)
-    for d in range(1, NZ):
+    for d in z_steps:
         m_copy(d, at_z(d)).start()
     for c in range(CHUNKS):
-        for d in range(1, NZ):
+        for d in z_steps:
             z_copy(c, 0, d, at_z(d)).start()
+
+    def core_copy(src, dst, send, get):
+        return pltpu.make_async_remote_copy(
+            src_ref=src, dst_ref=dst, send_sem=send, recv_sem=get, device_id=(me, other), device_id_type=MESH
+        )
+
+    shared = [core_copy(src, dst, w_s.at[i], w_r.at[i]) for i, (src, dst) in enumerate(pairs[5:8])]
+    for copy in shared:
+        copy.start()
 
     slot = lax.broadcasted_iota(jnp.int32, (slots, 1), 0)
     slot_o, slot_d, slot_s = slot // span, (slot // CAP) % NZ, slot % CAP
@@ -122,10 +148,9 @@
     block_base = NZ * plane * CAP
     slot_target = (slot_expert * CAP + slot_s + slot_d * block_base).astype(F32)
 
-    def plane_copy(c, src, dst, peer, o, send, get):
+    def plane_copy(src, dst, device, core, send, get):
         return pltpu.make_async_remote_copy(
-            src_ref=src.at[c, o], dst_ref=dst.at[c, o], send_sem=send, recv_sem=get,
-            device_id=(peer, sec), device_id_type=MESH,
+            src_ref=src, dst_ref=dst, send_sem=send, recv_sem=get, device_id=(device, core), device_id_type=MESH
         )
 
     m_copy(others, me).wait_recv()
@@ -136,9 +161,16 @@
         features = jnp.concatenate([zbuf[c, d // top] for d in range(NZ * top)], axis=0)
         chosen = jnp.dot(pick, features, preferred_element_type=F32).astype(BF).reshape(plane, span, cw)
         sel[c] = chosen
-        recv[c, 0] = chosen[0]
         for o, peer in forth:
-            plane_copy(c, sel, recv, peer, o, p_s.at[c], p_r.at[c]).start()
+            plane_copy(sel.at[c, o], recv.at[c, sec, o // 2], peer, o % 2, p_s.at[c], p_r.at[c]).start()
+
+        @pl.when(sec == 0)
+        def _():
+            pltpu.make_async_copy(sel.at[c, 0], recv.at[c, 0, 0], p_r.at[c]).start()
+
+        @pl.when(sec == 1)
+        def _():
+            plane_copy(sel.at[c, 0], recv.at[c, 1, 0], me, 0, e_s.at[c], p_r.at[c]).start()
 
     weighted = jnp.concatenate(
         [jnp.where(hit, mbuf[d, 1:2, :], 0.0) for d, hit in enumerate(hits)], axis=1
@@ -156,53 +188,66 @@
     vocabulary = tb.shape[0]
     column = jnp.zeros((rows, 1), jnp.int32)
     row_at = lax.broadcasted_iota(jnp.int32, (rows, 1), 0)
-    loads[13].wait()
+    loads[10].wait()
     for i in range(rows):
         column = jnp.where(row_at == i, codes[i], column)
     code_hit = (column == lax.broadcasted_iota(jnp.int32, (rows, vocabulary), 1)).astype(F32).astype(BF)
-    loads[11].wait()
+    loads[8].wait()
     emb[...] = jnp.dot(code_hit, tb[...], preferred_element_type=F32)
 
-    def core_copy(src, dst, send, get):
-        return pltpu.make_async_remote_copy(
-            src_ref=src, dst_ref=dst, send_sem=send, recv_sem=get, device_id=(me, other), device_id_type=MESH
-        )
-
-    everyone = pl.ds(1, plane - 1)
-    for i in range(5, 9):
+    for i in range(5, 8):
         loads[i].wait()
-    for c in range(CHUNKS):
-        plane_copy(c, sel, recv, me, everyone, p_s.at[c], p_r.at[c]).wait_recv()
-        core_copy(recv.at[c], part.at[c], f_s.at[c], f_r.at[c]).start()
-        product = jnp.dot(recv[c].reshape(slots, cw), wgu[0, c * cw : (c + 1) * cw, :], preferred_element_type=F32)
-        acc[...] = product if c == 0 else acc[...] + product
-    for c in range(CHUNKS):
-        core_copy(recv.at[c], part.at[c], f_s.at[c], f_r.at[c]).wait_recv()
-        acc[...] += jnp.dot(part[c].reshape(slots, cw), wgu[1, c * cw : (c + 1) * cw, :], preferred_element_type=F32)
-    gate_val = acc[:, 0:ff]
-    units = (gate_val / (1.0 + jnp.exp(-gate_val)) * acc[:, ff:]).astype(BF)
-
-    loads[9].wait()
-    for c in range(CHUNKS):
-        partial = jnp.dot(units, wd[1, :, c * cw : (c + 1) * cw], preferred_element_type=F32)
-        psend[c] = partial.astype(BF)
-        core_copy(psend.at[c], precv.at[c], q_s.at[c], q_r.at[c]).start()
-    loads[10].wait()
-    for c in range(CHUNKS):
-        own[c] = jnp.dot(units, wd[0, :, c * cw : (c + 1) * cw], preferred_element_type=F32)
-    for c in range(CHUNKS):
-        core_copy(psend.at[c], precv.at[c], q_s.at[c], q_r.at[c]).wait_recv()
-        finished = (own[c] + precv[c].astype(F32)).astype(BF).reshape(plane, span, cw)
-        outb[c] = finished
-        ret[c, 0] = finished[0]
-        for o, peer in back:
-            plane_copy(c, outb, ret, peer, o, r_s.at[c], r_r.at[c]).start()
+        shared[i - 5].wait_recv()
+    count = plane // 2
+    held = count * span
+    for c in range(CHUNKS):
+        plane_copy(recv.at[c], recv.at[c], me, other, p_s.at[c], p_r.at[c]).wait_recv()
+        for h in range(2):
+            at = h * half + c * cw
+            product = jnp.dot(recv[c, h].reshape(held, cw), wgu[at : at + cw, :], preferred_element_type=F32)
+            acc[...] = product if c + h == 0 else acc[...] + product
+    gate_val = acc[:, 0 : 2 * ff]
+    units = (gate_val / (1.0 + jnp.exp(-gate_val)) * acc[:, 2 * ff :]).astype(BF)
+
+    def offset_of(i):
+        return 2 * i + sec
+
+    def back_at(i):
+        return at_plane(NY - i // (NX // 2), NX - 2 * (i % (NX // 2)) - sec)
+
+    back = [(i, offset_of(i), back_at(i)) for i in range(1, count)]
+    back.sort(key=lambda entry: -2 * apart(entry[0] // (NX // 2), NY) - entry[0] % (NX // 2))
+    odd_home = back_at(0)
+    for c in range(CHUNKS):
+        for h in range(2):
+            at = h * half + c * cw
+            finished = jnp.dot(units, wd[:, at : at + cw], preferred_element_type=F32)
+            outb[c, h] = finished.astype(BF).reshape(count, span, cw)
+            for i, o, peer in back:
+                plane_copy(outb.at[c, h, i], ret.at[c, o], peer, h, r_s.at[c], r_r.at[c]).start()
+
+        @pl.when(sec == 0)
+        def _():
+            pltpu.make_async_copy(outb.at[c, 0, 0], ret.at[c, 0], r_r.at[c]).start()
+            plane_copy(outb.at[c, 1, 0], ret.at[c, 0], me, 1, g_s.at[c], r_r.at[c]).start()
+
+        @pl.when(sec == 1)
+        def _():
+            for h in range(2):
+                plane_copy(outb.at[c, h, 0], ret.at[c, 1], odd_home, h, g_s.at[c], r_r.at[c]).start()
 
     m_copy(others, me).wait_send()
     for c in range(CHUNKS):
         z_copy(c, others, others, me).wait_send()
-        plane_copy(c, sel, recv, me, everyone, p_s.at[c], p_r.at[c]).wait_send()
-        core_copy(recv.at[c], part.at[c], f_s.at[c], f_r.at[c]).wait_send()
+        sent = sel.at[c, pl.ds(1, plane - 1)]
+        plane_copy(sent, sent, me, other, p_s.at[c], p_r.at[c]).wait_send()
+
+        @pl.when(sec == 1)
+        def _():
+            plane_copy(sel.at[c, 0], recv.at[c, 1, 0], me, 0, e_s.at[c], p_r.at[c]).wait_send()
+
+    for copy in shared:
+        copy.wait_send()
 
     def u_copy(c, d, device):
         return pltpu.make_async_remote_copy(
@@ -211,15 +256,15 @@
         )
 
     for c in range(CHUNKS):
-        plane_copy(c, outb, ret, me, everyone, r_s.at[c], r_r.at[c]).wait_recv()
+        plane_copy(ret.at[c], ret.at[c], me, other, r_s.at[c], r_r.at[c]).wait_recv()
         both = jnp.dot(wmix[...], ret[c].reshape(slots, cw), preferred_element_type=F32)
         summed = (both[0:stream] + both[stream:]).astype(BF).reshape(NZ, rows, cw)
         zout[c] = summed
         zin[c, 0] = summed[0]
-        for d in range(1, NZ):
+        for d in z_steps:
             u_copy(c, d, at_z(NZ - d)).start()
 
-    loads[12].wait()
+    loads[9].wait()
     loads[4].wait()
     partial_talk = None
     for c in range(CHUNKS):
@@ -234,8 +279,18 @@
     talk_copy = core_copy(tsend, trecv, t_s, t_r)
     talk_copy.start()
     for c in range(CHUNKS):
-        core_copy(psend.at[c], precv.at[c], q_s.at[c], q_r.at[c]).wait_send()
-        plane_copy(c, outb, ret, me, everyone, r_s.at[c], r_r.at[c]).wait_send()
+        sent = outb.at[c, :, pl.ds(1, count - 1)]
+        plane_copy(sent, sent, me, other, r_s.at[c], r_r.at[c]).wait_send()
+
+        @pl.when(sec == 0)
+        def _():
+            plane_copy(outb.at[c, 1, 0], ret.at[c, 0], me, 1, g_s.at[c], r_r.at[c]).wait_send()
+
+        @pl.when(sec == 1)
+        def _():
+            sent = outb.at[c, :, 0]
+            plane_copy(sent, sent, me, other, g_s.at[c], r_r.at[c]).wait_send()
+
         u_copy(c, others, me).wait_send()
     talk_copy.wait()
 
@@ -277,6 +332,7 @@
     span, stream = NZ * CAP, NZ * rows
     slots = plane * span
     chunk = (CHUNKS, plane, span, cw)
+    by_core = (CHUNKS, 2, plane // 2, span, cw)
     dma = pltpu.SemaphoreType.DMA
     hbm = pl.BlockSpec(memory_space=pltpu.HBM)
     vmem = pl.BlockSpec(memory_space=pltpu.VMEM)
@@ -309,19 +365,15 @@
             pltpu.VMEM((top, rows), F32),
             pltpu.VMEM((1, width), F32),
             pltpu.VMEM((1, talk_width), F32),
-            pltpu.VMEM((2, half, 2 * ff), BF),
-            pltpu.VMEM((2, ff, half), BF),
+            pltpu.VMEM((width, 4 * ff), BF),
+            pltpu.VMEM((2 * ff, width), BF),
             pltpu.VMEM((half, talk_width), BF),
             pltpu.VMEM((NZ, 2, top * rows), F32),
             pltpu.VMEM((CHUNKS, NZ, rows, cw), BF),
             pltpu.VMEM(chunk, BF),
-            pltpu.VMEM(chunk, BF),
-            pltpu.VMEM(chunk, BF),
-            pltpu.VMEM((slots, 2 * ff), F32),
-            pltpu.VMEM((CHUNKS, slots, cw), BF),
-            pltpu.VMEM((CHUNKS, slots, cw), BF),
-            pltpu.VMEM((CHUNKS, slots, cw), F32),
-            pltpu.VMEM(chunk, BF),
+            pltpu.VMEM(by_core, BF),
+            pltpu.VMEM((slots // 2, 4 * ff), F32),
+            pltpu.VMEM(by_core, BF),
             pltpu.VMEM(chunk, BF),
             pltpu.VMEM((CHUNKS, NZ, rows, cw), BF),
             pltpu.VMEM((CHUNKS, NZ, rows, cw), BF),
@@ -329,7 +381,7 @@
             pltpu.VMEM((rows, talk_width), F32),
             pltpu.VMEM((rows, talk_width), F32),
             pltpu.VMEM((rows, talk_width), F32),
-            dma((14,)),
+            dma((11,)),
             dma,
             dma,
             dma((CHUNKS,)),
@@ -337,8 +389,8 @@
             dma((CHUNKS,)),
             dma((CHUNKS,)),
             dma((CHUNKS,)),
-            dma((CHUNKS,)),
-            dma((CHUNKS,)),
+            dma((3,)),
+            dma((3,)),
             dma((CHUNKS,)),
             dma((CHUNKS,)),
             dma((CHUNKS,)),
@@ -348,7 +400,7 @@
             dma,
         ],
         compiler_params=pltpu.CompilerParams(
-            collective_id=0, has_side_effects=True, vmem_limit_bytes=36 * 1024 * 1024
+            collective_id=0, has_side_effects=True, vmem_limit_bytes=40 * 1024 * 1024
         ),
         name="expert_step",
     )(*[pltpu.with_memory_space_constraint(operand, pltpu.HBM) for operand in operands])

time: 46.9 us -> 44.2 us (0.942)
  Pallas kernels: 46.2 us -> 43.5 us
    pallas_call x1, Pallas kernels: 44.3 us -> 41.6 us  [shards(): pl.pallas_call(kernel, out_shape=(pltpu.VMEM((rows, half), BF), pltpu.VME...]
where the time goes in v3:
time: 44.2 us; the launch traced here: 44.1 us
  Pallas kernels  43.5 us (98%)
  between operations  0.64 us (1%)
    pallas_call x1, Pallas kernels, shards(): pl.pallas_call(kernel, out_shape=(pltpu.VMEM((rows, half), BF), pltpu.VME...  41.6 us
    pallas_call x1, Pallas kernels, shards(): pl.pallas_call(head, out_shape=(jax.ShapeDtypeStruct((rows, half), BF), j...  1.85 us

profile of v3, /device:TPU:1, one launch (start us, length us, event | category | flops | bytes accessed | tf_op | source)
XLA Modules:
  0.0 44.1 jit_solution(7538365506616034221)
XLA Ops:
  0.6 41.6 %expert_step.1 = (bf16[16,1024]{1,0:T(8,128)(2,1)S(1)}, bf16[16,1024]{1,0:T(8,128)(2,1)S(1)}, bf16[2048,1024]{1,0:T(8,128)(2,1)S(1)}) custom-call(bf16[16,2048]{1,0:T(8,128)(2,1)} %tokens_hbm.1, s32[8,16]{1,0:T(8,128)} %bitcast.5, f32[8,16]{1,0:T(8,128)} %bitcast.6, f32[1,2048]{1,0:T(1,128)} %bitcast.4, bf16[1,2048,384]{2,1,0:T(8,128)(2,1)} %gate_hbm.1, ...), custom_call_target="tpu_custom_call" | custom-call | tf_op jit(solution)/shard_map/expert_step/pallas_call | solution.py:352
  42.3 1.9 %head.1 = (bf16[16,1024]{1,0:T(8,128)(2,1)}, bf16[16,2048]{1,0:T(8,128)(2,1)}) custom-call(bf16[16,1024]{1,0:T(8,128)(2,1)S(1)} %get-tuple-element.7.hidden, bf16[16,1024]{1,0:T(8,128)(2,1)S(1)} %get-tuple-element.8.level_normed, bf16[2048,1024]{1,0:T(8,128)(2,1)S(1)} %get-tuple-element.9.table), custom_call_target="tpu_custom_call" | custom-call | tf_op jit(solution)/shard_map/head/pallas_call | solution.py:407

commit v4 on v3

--- a/solution.py
+++ b/solution.py
@@ -16,8 +16,8 @@
 
 def kernel(
     tokens_hbm, routes_hbm, weight_hbm, gain_hbm, gate_hbm, up_hbm, down_hbm, proj_hbm, table_hbm, lgain_hbm, codes_hbm,
-    hidden_out, level_out, tb,
-    codes, tok, rts, rwt, gain, lgain, wgu, wd, wp,
+    hidden_out, level_out, across_out,
+    tb, codes, tok, rts, rwt, gain, lgain, wgu, wd, wp,
     mbuf, zbuf, sel, recv, acc, outb, ret, zout, zin, wmix, emb, tsend, trecv,
     load_sem, m_s, m_r, z_s, z_r, p_s, p_r, e_s, w_s, w_r, r_s, r_r, g_s, u_s, u_r, t_s, t_r,
 ):
@@ -195,6 +195,10 @@
     loads[8].wait()
     emb[...] = jnp.dot(code_hit, tb[...], preferred_element_type=F32)
 
+    strip = vocabulary // 8
+    for i in range(8):
+        across_out[:, i * strip : (i + 1) * strip] = tb[i * strip : (i + 1) * strip, :].T
+
     for i in range(5, 8):
         loads[i].wait()
         shared[i - 5].wait_recv()
@@ -302,8 +306,8 @@
 def head(hidden, level_normed, table, hidden_hbm, logits_hbm, logits, sems):
     hidden_copy = pltpu.make_async_copy(hidden, hidden_hbm, sems.at[0])
     hidden_copy.start()
-    scores = lax.dot_general(level_normed[...], table[...], (((1,), (1,)), ((), ())), preferred_element_type=F32)
-    logits[...] = (scores / (table.shape[1] ** 0.5)).astype(BF)
+    scores = jnp.dot(level_normed[...], table[...], preferred_element_type=F32)
+    logits[...] = (scores / (table.shape[0] ** 0.5)).astype(BF)
     logits_copy = pltpu.make_async_copy(logits, logits_hbm, sems.at[1])
     logits_copy.start()
     hidden_copy.wait()
@@ -354,11 +358,12 @@
         out_shape=(
             pltpu.VMEM((rows, half), BF),
             pltpu.VMEM((rows, talk_width), BF),
-            pltpu.VMEM((vocabulary, talk_width), BF),
+            pltpu.VMEM((talk_width, vocabulary), BF),
         ),
         in_specs=[hbm] * 11,
         out_specs=(vmem,) * 3,
         scratch_shapes=[
+            pltpu.VMEM((vocabulary, talk_width), BF),
             pltpu.SMEM((rows,), jnp.int32),
             pltpu.VMEM((rows, width), BF),
             pltpu.VMEM((top, rows), jnp.int32),
@@ -400,7 +405,7 @@
             dma,
         ],
         compiler_params=pltpu.CompilerParams(
-            collective_id=0, has_side_effects=True, vmem_limit_bytes=40 * 1024 * 1024
+            collective_id=0, has_side_effects=True, vmem_limit_bytes=44 * 1024 * 1024
         ),
         name="expert_step",
     )(*[pltpu.with_memory_space_constraint(operand, pltpu.HBM) for operand in operands])

time: 44.2 us -> 43.7 us (0.989)
  Pallas kernels: 43.5 us -> 42.9 us
    pallas_call x1, Pallas kernels: 1.85 us -> 1.31 us  [shards(): pl.pallas_call(head, out_shape=(jax.ShapeDtypeStruct((rows, half), BF), j...]
where the time goes in v4:
time: 43.7 us; the launch traced here: 43.6 us
  Pallas kernels  42.9 us (98%)
  between operations  0.64 us (1%)
    pallas_call x1, Pallas kernels, shards(): pl.pallas_call(kernel, out_shape=(pltpu.VMEM((rows, half), BF), pltpu.VME...  41.6 us
    pallas_call x1, Pallas kernels, shards(): pl.pallas_call(head, out_shape=(jax.ShapeDtypeStruct((rows, half), BF), j...  1.31 us

profile of v4, /device:TPU:1, one launch (start us, length us, event | category | flops | bytes accessed | tf_op | source)
XLA Modules:
  0.0 43.6 jit_solution(12092780628044154168)
XLA Ops:
  0.6 41.6 %expert_step.1 = (bf16[16,1024]{1,0:T(8,128)(2,1)S(1)}, bf16[16,1024]{1,0:T(8,128)(2,1)S(1)}, bf16[1024,2048]{1,0:T(8,128)(2,1)S(1)}) custom-call(bf16[16,2048]{1,0:T(8,128)(2,1)} %tokens_hbm.1, s32[8,16]{1,0:T(8,128)} %bitcast.5, f32[8,16]{1,0:T(8,128)} %bitcast.6, f32[1,2048]{1,0:T(1,128)} %bitcast.4, bf16[1,2048,384]{2,1,0:T(8,128)(2,1)} %gate_hbm.1, ...), custom_call_target="tpu_custom_call" | custom-call | tf_op jit(solution)/shard_map/expert_step/pallas_call | solution.py:356
  42.3 1.3 %head.1 = (bf16[16,1024]{1,0:T(8,128)(2,1)}, bf16[16,2048]{1,0:T(8,128)(2,1)}) custom-call(bf16[16,1024]{1,0:T(8,128)(2,1)S(1)} %get-tuple-element.7.hidden, bf16[16,1024]{1,0:T(8,128)(2,1)S(1)} %get-tuple-element.8.level_normed, bf16[1024,2048]{1,0:T(8,128)(2,1)S(1)} %get-tuple-element.9.table), custom_call_target="tpu_custom_call" | custom-call | tf_op jit(solution)/shard_map/head/pallas_call | solution.py:412

commit v5 on v4

--- a/solution.py
+++ b/solution.py
@@ -156,9 +156,13 @@
     m_copy(others, me).wait_recv()
     hits = [mbuf[d, 0:1, :] + float(d * block_base) == slot_target for d in range(NZ)]
     pick = jnp.concatenate([hit.astype(F32).astype(BF) for hit in hits], axis=1)
+    pair = lax.broadcasted_iota(jnp.int32, (pairs_all, stream), 0)
+    row_of = (pair // named) * rows + pair % rows
+    fold = (row_of == lax.broadcasted_iota(jnp.int32, (pairs_all, stream), 1)).astype(F32).astype(BF)
+    pick = jnp.dot(pick, fold, preferred_element_type=F32).astype(BF)
     for c in range(CHUNKS):
         z_copy(c, others, others, me).wait_recv()
-        features = jnp.concatenate([zbuf[c, d // top] for d in range(NZ * top)], axis=0)
+        features = zbuf[c].reshape(stream, cw)
         chosen = jnp.dot(pick, features, preferred_element_type=F32).astype(BF).reshape(plane, span, cw)
         sel[c] = chosen
         for o, peer in forth:
@@ -177,9 +181,6 @@
     )
     weighted_hi = weighted.astype(BF)
     weighted_lo = (weighted - weighted_hi.astype(F32)).astype(BF)
-    pair = lax.broadcasted_iota(jnp.int32, (pairs_all, stream), 0)
-    row_of = (pair // named) * rows + pair % rows
-    fold = (row_of == lax.broadcasted_iota(jnp.int32, (pairs_all, stream), 1)).astype(F32).astype(BF)
     across = jnp.dot(weighted_hi, fold, preferred_element_type=F32).T
     wmix[0:stream] = across.astype(BF)
     across = jnp.dot(weighted_lo, fold, preferred_element_type=F32).T
@@ -206,10 +207,10 @@
     held = count * span
     for c in range(CHUNKS):
         plane_copy(recv.at[c], recv.at[c], me, other, p_s.at[c], p_r.at[c]).wait_recv()
-        for h in range(2):
-            at = h * half + c * cw
-            product = jnp.dot(recv[c, h].reshape(held, cw), wgu[at : at + cw, :], preferred_element_type=F32)
-            acc[...] = product if c + h == 0 else acc[...] + product
+        product = jnp.dot(recv[c, 0].reshape(held, cw), wgu[c * cw : (c + 1) * cw, :], preferred_element_type=F32)
+        at = half + c * cw
+        product += jnp.dot(recv[c, 1].reshape(held, cw), wgu[at : at + cw, :], preferred_element_type=F32)
+        acc[...] = product if c == 0 else acc[...] + product
     gate_val = acc[:, 0 : 2 * ff]
     units = (gate_val / (1.0 + jnp.exp(-gate_val)) * acc[:, 2 * ff :]).astype(BF)
 

time: 43.7 us -> 43.5 us (level)
  no operation moved by 1% of the time
where the time goes in v5:
time: 43.5 us; the launch traced here: 43.4 us
  Pallas kernels  42.7 us (98%)
  between operations  0.64 us (1%)
    pallas_call x1, Pallas kernels, shards(): pl.pallas_call(kernel, out_shape=(pltpu.VMEM((rows, half), BF), pltpu.VME...  41.4 us
    pallas_call x1, Pallas kernels, shards(): pl.pallas_call(head, out_shape=(jax.ShapeDtypeStruct((rows, half), BF), j...  1.31 us

profile of v5, /device:TPU:1, one launch (start us, length us, event | category | flops | bytes accessed | tf_op | source)
XLA Modules:
  0.0 43.4 jit_solution(942455203148638189)
XLA Ops:
  0.6 41.4 %expert_step.1 = (bf16[16,1024]{1,0:T(8,128)(2,1)S(1)}, bf16[16,1024]{1,0:T(8,128)(2,1)S(1)}, bf16[1024,2048]{1,0:T(8,128)(2,1)S(1)}) custom-call(bf16[16,2048]{1,0:T(8,128)(2,1)} %tokens_hbm.1, s32[8,16]{1,0:T(8,128)} %bitcast.5, f32[8,16]{1,0:T(8,128)} %bitcast.6, f32[1,2048]{1,0:T(1,128)} %bitcast.4, bf16[1,2048,384]{2,1,0:T(8,128)(2,1)} %gate_hbm.1, ...), custom_call_target="tpu_custom_call" | custom-call | tf_op jit(solution)/shard_map/expert_step/pallas_call | solution.py:357
  42.1 1.3 %head.1 = (bf16[16,1024]{1,0:T(8,128)(2,1)}, bf16[16,2048]{1,0:T(8,128)(2,1)}) custom-call(bf16[16,1024]{1,0:T(8,128)(2,1)S(1)} %get-tuple-element.7.hidden, bf16[16,1024]{1,0:T(8,128)(2,1)S(1)} %get-tuple-element.8.level_normed, bf16[1024,2048]{1,0:T(8,128)(2,1)S(1)} %get-tuple-element.9.table), custom_call_target="tpu_custom_call" | custom-call | tf_op jit(solution)/shard_map/head/pallas_call | solution.py:413
